TPU v7x, 512 devices: a whole 4x4x16 slice. The times are simulated.
512 devices in a mesh: tm: 16 (over z_hi, y, core), row: 4 (over x), col: 8 (over z_lo).
Axes of the slice: x: 4, y: 4, z: 16 (z_hi: 2, z_lo: 8; z = z_hi * 8 + z_lo), core: 2. Of those that a mesh axis runs over, the one named last changes fastest.
Arguments:
- particles: float32 [16, 8192, 256], P('tm', ('row', 'col')), may hold values from -6 to 6
- source_pots: float32 [16, 8192], P('tm', ('row', 'col')), may hold values from 0.85 to 1.15
- target_pots: float32 [16, 8192], P('tm', ('row', 'col')), may hold values from 0.85 to 1.15
Outputs:
- gradient: float32 [16, 8192, 256], P('tm', ('row', 'col'))
All inputs are finite; a program needn't handle non-finite values.
Results may differ from a plain program's by a relative error of at most 0.0003.
Values sent between devices are 32-bit elements; how exact they have to be, the bound alone decides.
A program may use at most 64 MiB of HBM per device.

v0:
```python
import jax
import jax.numpy as jnp
from jax import lax
from jax.sharding import PartitionSpec as P

EPS = 0.1


def from_behind(x, axis, by):
    length = lax.axis_size(axis)
    pairs = [(i, i + by) for i in range(length) if 0 <= i + by < length]
    return lax.ppermute(x, axis, pairs)


def tile_terms(row_points, row_pots, col_points, col_pots, population):
    features = row_points.shape[1]
    row_norms = jnp.sum(row_points * row_points, axis=1)
    col_norms = jnp.sum(col_points * col_points, axis=1)
    crossed = lax.dot_general(
        row_points,
        col_points,
        (((1,), (1,)), ((), ())),
        precision=lax.Precision.HIGHEST,
        preferred_element_type=jnp.float32,
    )
    distance = (row_norms[:, None] + col_norms[None, :] - 2.0 * crossed) / features
    weights = jnp.exp((row_pots[:, None] + col_pots[None, :] - distance) / EPS) / population
    source = jnp.sum(weights, axis=1)[:, None] * row_points - jnp.dot(
        weights, col_points, precision=lax.Precision.HIGHEST, preferred_element_type=jnp.float32
    )
    target = jnp.sum(weights, axis=0)[:, None] * col_points - lax.dot_general(
        weights,
        row_points,
        (((0,), (0,)), ((), ())),
        precision=lax.Precision.HIGHEST,
        preferred_element_type=jnp.float32,
    )
    return (source, target)


def local(particles, source_pots, target_pots):
    own_points = particles[0]
    own_source = source_pots[0]
    own_target = target_pots[0]
    own_rows, features = own_points.shape
    rows_across = lax.axis_size("row")
    cols_across = lax.axis_size("col")
    times_across = lax.axis_size("tm")
    population = own_rows * rows_across * cols_across
    col_points, col_pots = (
        lax.all_gather(own_points, "row", axis=0, tiled=True),
        lax.all_gather(own_target, "row", axis=0, tiled=True),
    )
    col_points, col_pots = from_behind((col_points, col_pots), "tm", -1)
    source, target = tile_terms(
        lax.all_gather(own_points, "col", axis=0, tiled=True),
        lax.all_gather(own_source, "col", axis=0, tiled=True),
        col_points,
        col_pots,
        population,
    )
    source_rows = source
    active = lax.axis_index("tm") < times_across - 1
    source_rows = jnp.where(active, source_rows, jnp.zeros_like(source_rows))
    summed = lax.psum(source_rows, "col")
    own_grad = lax.dynamic_slice_in_dim(summed, lax.axis_index("col") * own_rows, own_rows, 0)
    arrived = from_behind(target, "tm", 1)
    incoming = lax.psum_scatter(arrived, "row", scatter_dimension=0, tiled=True)
    return (own_grad + incoming)[None]


def solution(mesh):
    in_specs = (P("tm", ("row", "col"), None), P("tm", ("row", "col")), P("tm", ("row", "col")))
    out_specs = P("tm", ("row", "col"), None)
    return jax.shard_map(local, mesh=mesh, in_specs=in_specs, out_specs=out_specs, check_vma=False)
```

profile of v0, /device:TPU:448, one launch (start us, length us, event | category | flops | bytes accessed | tf_op | source)
XLA Modules:
  0.0 379.1 jit_solution(12094868667238749953)
XLA Ops:
  6.5 0.0 all-gather.9.cloned.1.call-start
  6.5 0.7 all-gather.9.cloned.1.call-update
  7.3 0.0 all-gather.7.cloned.1.call-start
  7.3 0.7 all-gather.7.cloned.1.call-update
  8.0 0.0 all-reduce.2.cloned.1.call-start
  8.1 32.4 %all-gather.9.cloned.1.call-done = f32[1,1024,256]{2,1,0:T(8,128)} async-done(((f32[1,256,256]{2,1,0:T(8,128)}), f32[1,1024,256]{2,1,0:T(8,128)}) %all-gather.9.cloned.1.call-update) | async-done | bytes 1048592 | tf_op jit(solution)/shard_map/all_gather | solution.py:51
  40.5 9.0 %collective-permute-start.1 = (f32[1024,256]{1,0:T(8,128)}, f32[1024,256]{1,0:T(8,128)S(1)}, u32[]{:S(2)}, u32[]{:S(2)}) collective-permute-start(f32[1024,256]{1,0:T(8,128)} %bitcast.28), channel_id=1, source_target_pairs={{32,0},{64,32},{96,64},{128,96},{160,128},{192,160},{224,192},{256... | collective-permute-start | bytes 3145736 | tf_op jit(solution)/shard_map/ppermute | solution.py:12
  49.5 8.7 %all-gather.1 = f32[1,1024]{1,0:T(1,128)S(1)} all-gather(f32[1,256]{1,0:T(1,128)} %param.5), channel_id=3, replica_groups=mesh['tm'=16,'row'=4,'col'=8] {'row'}, dimensions={1}, use_global_device_ids=true | all-gather | bytes 5120 | tf_op jit(solution)/shard_map/all_gather | solution.py:52
  58.3 1.9 collective-permute-start
  60.2 83.8 %all-gather = f32[1,2048]{1,0:T(1,128)S(1)} all-gather(f32[1,256]{1,0:T(1,128)} %param.4), channel_id=2, replica_groups=mesh['tm'=16,'row'=4,'col'=8] {'col'}, dimensions={1}, use_global_device_ids=true | all-gather | bytes 9216 | tf_op jit(solution)/shard_map/all_gather | solution.py:57
  144.0 0.0 collective-permute-done.1
  144.0 0.2 multiply_reduce_fusion
  144.2 0.0 all-gather.7.cloned.1.call-done
  144.2 1.9 fusion.3
  146.1 0.0 collective-permute-done
  146.2 0.0 copy-start.1
  146.2 12.3 %fusion.6 = (f32[2048]{0:T(1024)S(1)}, f32[1024]{0:T(1024)S(1)}, f32[2048,1024]{1,0:T(8,128)S(1)}) fusion(f32[1024,256]{1,0:T(8,128)S(1)} %collective-permute-done.1, f32[1,2048,256]{2,1,0:T(8,128)} %all-gather.7.cloned.1.call-done, f32[1024]{0:T(1024)S(1)} %multiply_reduce_fusion, f32[2048]{0:T(1024)S(1)} %fusion.3, f32[1024]{0:T(1024)S(1)} %collective-permute-done, ...), kind=kOutput, calls=%fused_computation.12 | convolution fusion | flops 6463419392 | bytes 11571200 | tf_op jit(solution)/shard_map/dot_general | solution.py:19
  158.5 0.0 copy-start
  158.5 3.2 copy-done
  161.7 0.0 copy-done.1
  161.7 8.4 %fusion.5 = f32[2048,256]{1,0:T(8,128)} fusion(f32[1,2048,256]{2,1,0:T(8,128)S(1)} %copy-done.1, f32[2048]{0:T(1024)S(1)} %get-tuple-element.5, pred[]{:T(512)S(6)} %lt.6, f32[2048,1024]{1,0:T(8,128)S(1)} %get-tuple-element.7, f32[1024,256]{1,0:T(8,128)S(1)} %collective-permute-done.1), kind=kOutput, calls=%fused_computation.8 | convolution fusion | flops 6444023808 | bytes 13639681 | tf_op jit(solution)/shard_map/dot_general | solution.py:28
  170.0 0.0 all-reduce.2.cloned.1.call-update
  170.1 0.0 reduce-scatter.2.cloned.1.call-start
  170.1 15.9 %multiply_subtract_fusion = f32[1024,256]{1,0:T(8,128)S(1)} fusion(f32[1024,256]{1,0:T(8,128)S(1)} %collective-permute-done.1, f32[1024]{0:T(1024)S(1)} %get-tuple-element.6, f32[2048,1024]{1,0:T(8,128)} %copy-done, f32[1,2048,256]{2,1,0:T(8,128)S(1)} %copy-done.1), kind=kOutput, calls=%fused_computation.9 | convolution fusion | flops 6442975232 | bytes 12587008 | tf_op jit(solution)/shard_map/dot_general | solution.py:31
  186.0 1.9 collective-permute-start.2
  188.0 79.1 %collective-permute-done.2 = f32[1024,256]{1,0:T(8,128)S(1)} collective-permute-done((f32[1024,256]{1,0:T(8,128)S(1)}, f32[1024,256]{1,0:T(8,128)S(1)}, u32[]{:S(2)}, u32[]{:S(2)}) %collective-permute-start.2) | collective-permute-done | bytes 1048608 | tf_op jit(solution)/shard_map/ppermute | solution.py:12
  267.0 0.0 copy-start.2
  267.0 1.0 copy-done.2
  268.0 0.0 reduce-scatter.2.cloned.1.call-update
  268.0 68.4 %all-reduce.2.cloned.1.call-done = f32[2048,256]{1,0:T(8,128)} async-done(((f32[2048,256]{1,0:T(8,128)}), f32[2048,256]{1,0:T(8,128)}) %all-reduce.2.cloned.1.call-update) | async-done | bytes 2097168 | tf_op jit(solution)/shard_map/psum | solution.py:65
  336.4 34.4 %reduce-scatter.2.cloned.1.call-done = f32[256,256]{1,0:T(8,128)} async-done(((f32[1024,256]{1,0:T(8,128)}), f32[256,256]{1,0:T(8,128)}) %reduce-scatter.2.cloned.1.call-update) | async-done | bytes 262160 | tf_op jit(solution)/shard_map/reduce_scatter | solution.py:68
  370.8 1.8 add_bitcast_fusion
Async XLA Ops:
  6.5 34.0 %all-gather.9.cloned.1.call-start = ((), (), s32[]{:S(2)}) async-start(), calls=%async_computation.4 | async-start | bytes 1310720 | tf_op jit(solution)/shard_map/all_gather | solution.py:51
  7.3 136.9 %all-gather.7.cloned.1.call-start = ((), (), s32[]{:S(2)}) async-start(), calls=%async_computation.3 | async-start | bytes 2359296 | tf_op jit(solution)/shard_map/all_gather | solution.py:56
  8.0 328.4 %all-reduce.2.cloned.1.call-start = ((), (), s32[]{:S(2)}) async-start(), calls=%async_computation.1 | async-start | bytes 4194304 | tf_op jit(solution)/shard_map/psum | solution.py:65
  40.5 103.5 %collective-permute-start.1 = (f32[1024,256]{1,0:T(8,128)}, f32[1024,256]{1,0:T(8,128)S(1)}, u32[]{:S(2)}, u32[]{:S(2)}) collective-permute-start(f32[1024,256]{1,0:T(8,128)} %bitcast.28), channel_id=1, source_target_pairs={{32,0},{64,32},{96,64},{128,96},{160,128},{192,160},{224,192},{256... | collective-permute-start | bytes 3145736 | tf_op jit(solution)/shard_map/ppermute | solution.py:12
  58.3 87.9 %collective-permute-start = (f32[1024]{0:T(1024)S(1)}, f32[1024]{0:T(1024)S(1)}, u32[]{:S(2)}, u32[]{:S(2)}) collective-permute-start(f32[1024]{0:T(1024)S(1)} %bitcast.27), channel_id=1, source_target_pairs={{32,0},{64,32},{96,64},{128,96},{160,128},{192,160},{224,192},{256... | collective-permute-start | bytes 12296 | tf_op jit(solution)/shard_map/ppermute | solution.py:12
  146.2 15.5 %copy-start.1 = (f32[1,2048,256]{2,1,0:T(8,128)S(1)}, f32[1,2048,256]{2,1,0:T(8,128)}, u32[]{:S(2)}) copy-start(f32[1,2048,256]{2,1,0:T(8,128)} %all-gather.7.cloned.1.call-done) | copy-start | bytes 6291460
  158.5 3.2 copy-start
  170.1 200.8 %reduce-scatter.2.cloned.1.call-start = ((), (), s32[]{:S(2)}) async-start(), calls=%async_computation.2 | async-start | bytes 1310720 | tf_op jit(solution)/shard_map/reduce_scatter | solution.py:68
  186.0 81.0 %collective-permute-start.2 = (f32[1024,256]{1,0:T(8,128)S(1)}, f32[1024,256]{1,0:T(8,128)S(1)}, u32[]{:S(2)}, u32[]{:S(2)}) collective-permute-start(f32[1024,256]{1,0:T(8,128)S(1)} %multiply_subtract_fusion), channel_id=1, source_target_pairs={{0,32},{32,64},{64,96},{96,128},{128,160},{160,192},{192,224},{224... | collective-permute-start | bytes 3145736 | tf_op jit(solution)/shard_map/ppermute | solution.py:12
  267.0 1.0 copy-start.2
Sparse Core Ops, SparseCore 0:
  9.5 30.9 all-gather.8
  42.6 90.6 all-gather.6
  170.2 166.2 all-reduce.1
  339.1 31.6 reduce-scatter.1
where the time goes:
time: 384 us; the launch traced here: 379 us
  waiting for transfers between devices  216 us (56%)
  blocking collectives  92.5 us (24%)
  matrix products  36.6 us (10%)
  between operations  13.2 us (3%)
  starting transfers between devices  13 us (3%)
  local copies, waits for them, and re-layouts  4.19 us (1%)
  other arithmetic  3.91 us (1%)
    all_gather x1, blocking collectives, local(): lax.all_gather(own_source, 'col', axis=0, tiled=True)  83.8 us
    ppermute x3, waiting for transfers between devices, from_behind(): return lax.ppermute(x, axis, pairs)  79.1 us
    psum x1, waiting for transfers between devices, local(): summed = lax.psum(source_rows, 'col')  68.4 us
    reduce_scatter x1, waiting for transfers between devices, local(): incoming = lax.psum_scatter(arrived, 'row', scatter_dimension=0, tiled=True)  34.4 us
    all_gather x1, waiting for transfers between devices, local(): lax.all_gather(own_points, 'row', axis=0, tiled=True)  32.4 us
    dot_general x1, matrix products, tile_terms(): lax.dot_general(weights, row_points, (((0,), (0,)), ((), ())), precision=...  15.9 us
    ppermute x3, starting transfers between devices, from_behind(): return lax.ppermute(x, axis, pairs)  12.9 us
    dot_general x1, matrix products, tile_terms(): lax.dot_general(row_points, col_points, (((1,), (1,)), ((), ())), precisi...  12.3 us
  transfers between devices with their start and end apart: 7, of which 4 were waited for; matrix products, arithmetic and copies ran while one was open for 5% of the time, Pallas kernels for 0%

commit v1 on v0

v1 whole, which is shorter than its diff:
```python
import functools
import math

import jax
import jax.numpy as jnp
from jax import lax
from jax.experimental import pallas as pl
from jax.experimental.pallas import tpu as pltpu
from jax.sharding import PartitionSpec as P

EPS = 0.1
MESH = pl.DeviceIdType.MESH
F32 = jnp.float32
BF16 = jnp.bfloat16


def split(x):
    hi = x.astype(BF16)
    return hi, (x - hi.astype(F32)).astype(BF16)


def dot(a, b, dims):
    return lax.dot_general(a, b, (dims, ((), ())), preferred_element_type=F32)


def dot3(a, b, dims):
    return dot(a[0], b[0], dims) + dot(a[0], b[1], dims) + dot(a[1], b[0], dims)


def eye(n):
    return lax.broadcasted_iota(jnp.int32, (n, n), 0) == lax.broadcasted_iota(jnp.int32, (n, n), 1)


def to_row(col):
    n = col.shape[0]
    return jnp.sum(jnp.where(eye(n), col, 0.0), axis=0, keepdims=True)


def to_col(row):
    n = row.shape[1]
    return jnp.sum(jnp.where(eye(n), row, 0.0), axis=1, keepdims=True)


def kernel(
    dims,
    pts_ref,
    spot_ref,
    tpot_ref,
    out_ref,
    sbuf,
    mbuf,
    mhi,
    mlo,
    brow,
    part,
    sib_part,
    right_sum,
    left_sum,
    gmt,
    csum,
    gm,
    gm_in,
    gtm_in,
    fin,
    zr_s,
    zr_r,
    zl_s,
    zl_r,
    sib_s,
    sib_r,
    own_s,
    own_r,
    tm_s,
    tm_r,
    mx_s,
    mx_r,
    pe_s,
    pe_r,
    cr_s,
    cr_r,
    cl_s,
    cl_r,
    gm_s,
    gm_r,
    gt_s,
    gt_r,
    fin_s,
    fin_r,
):
    times, nx, nz, rows, feats = dims
    half = rows // 2
    hrow = half + 8
    last = nz - 1
    population = rows * nx * nz
    scale = math.log2(math.e) / EPS
    tm, x, z = lax.axis_index("tm"), lax.axis_index("row"), lax.axis_index("col")
    core = lax.rem(tm, 2)
    is0, is1 = core == 0, core == 1
    active = tm < times - 1
    fed = jnp.logical_and(is1, active)
    feeds = jnp.logical_and(is0, tm > 0)
    has_left, has_right = z > 0, z < last
    sib = (tm + 1 - 2 * core, x, z)
    zright, zleft = (tm, x, jnp.minimum(z + 1, last)), (tm, x, jnp.maximum(z - 1, 0))
    before, after = (jnp.maximum(tm - 1, 0), x, z), (jnp.minimum(tm + 1, times - 1), x, z)
    xs = [(tm, lax.rem(x + 1 + k, nx), z) for k in range(nx - 1)]

    def rdma(src, dst, s, r, to):
        return pltpu.make_async_remote_copy(
            src_ref=src, dst_ref=dst, send_sem=s, recv_sem=r, device_id=to, device_id_type=MESH
        )

    barrier = pltpu.get_barrier_semaphore()

    def greet(to):
        pl.semaphore_signal(barrier, inc=1, device_id=to, device_id_type=MESH)

    greet(sib)
    for to in xs:
        greet(to)
    pl.when(has_left)(lambda: greet(zleft))
    pl.when(has_right)(lambda: greet(zright))
    pl.when(feeds)(lambda: greet(before))
    pl.when(fed)(lambda: greet(after))

    pts = pts_ref[...]
    norm = to_row(jnp.sum(pts * pts, axis=1, keepdims=True)) * (scale / feats)
    trow = tpot_ref[...] * scale - norm
    srow = spot_ref[...] * scale - norm - math.log2(population)

    def put(buf, b):
        for h in range(2):
            buf[b, h * hrow : h * hrow + half, :] = pts[h * half : (h + 1) * half]
            pair = jnp.concatenate(
                [trow[:, h * half : (h + 1) * half], srow[:, h * half : (h + 1) * half], jnp.zeros((6, half), F32)], axis=0
            )
            buf[b, h * hrow + half : (h + 1) * hrow, :] = jnp.concatenate(
                [pair, jnp.zeros((8, feats - half), F32)], axis=1
            )

    pl.when(is0)(lambda: put(mbuf, x))
    pl.when(is1)(lambda: put(sbuf, z))
    gmt[...] = jnp.zeros_like(gmt)
    csum[...] = jnp.zeros_like(csum)

    partners = nx + has_left.astype(jnp.int32) + has_right.astype(jnp.int32)
    partners = partners + feeds.astype(jnp.int32) + fed.astype(jnp.int32)
    pl.semaphore_wait(barrier, partners)

    mine = pl.ds(pl.multiple_of(core * hrow, 8), hrow)
    other = pl.ds(pl.multiple_of((1 - core) * hrow, 8), hrow)

    def own_copy(h):
        ref = sbuf.at[z, pl.ds(h * hrow, hrow)]
        return rdma(ref, ref, own_s.at[h], own_r.at[h], sib)

    def tm_copy():
        return rdma(mbuf.at[x], mbuf.at[x], tm_s, tm_r, before)

    def mx_copy(k):
        return rdma(mbuf.at[x], mbuf.at[x], mx_s.at[k], mx_r.at[k], xs[k])

    def mx_arrival(k):
        ref = mbuf.at[lax.rem(x + nx - 1 - k, nx)]
        return rdma(ref, ref, mx_s.at[k], mx_r.at[k], xs[k])

    @pl.when(is1)
    def _():
        own_copy(0).start()
        own_copy(1).start()

    @pl.when(is0)
    def _():
        pl.when(feeds)(lambda: tm_copy().start())
        for k in range(nx - 1):
            mx_copy(k).start()
        own_copy(0).wait_recv()

    def zr_copy(s, b):
        ref = sbuf.at[b, mine]
        return rdma(ref, ref, zr_s.at[s], zr_r.at[s], zright)

    def zl_copy(s, b):
        ref = sbuf.at[b, mine]
        return rdma(ref, ref, zl_s.at[s], zl_r.at[s], zleft)

    def sib_copy(b, window):
        ref = sbuf.at[b, window]
        return rdma(ref, ref, sib_s.at[b], sib_r.at[b], sib)

    cross = tm == times // 2 - 1
    wait_m = jnp.where(cross, nz, 1)
    first = jnp.where(is0, 2, wait_m + 1)

    def order(n):
        low = jnp.minimum(z, last - z)
        d = (n + 1) // 2
        near = z + jnp.where(lax.rem(n, 2) == 1, -d, d)
        far = jnp.where(z < nz - nz // 2, n, last - n)
        return jnp.where(n <= 2 * low, near, far)

    mine_rows = pl.ds(pl.multiple_of(core * half, 8), half)
    other_rows = pl.ds(pl.multiple_of((1 - core) * half, 8), half)

    def pe_copy(b, window):
        return rdma(part.at[b, window], sib_part.at[b], pe_s.at[b], pe_r.at[b], sib)

    def prepare():
        for k in range(nx - 1):
            mx_arrival(k).wait_recv()
        for j in range(nx):
            for h in range(2):
                at = j * rows + h * half
                hi, lo = split(mbuf[j, h * hrow : h * hrow + half, :])
                mhi[at : at + half, :] = hi
                mlo[at : at + half, :] = lo
                pair = mbuf[j, h * hrow + half : (h + 1) * hrow, 0:half]
                brow[0:1, at : at + half] = jnp.where(is0, pair[1:2], pair[0:1])

    def tile(b):
        pieces, cols = [], []
        for h in range(2):
            pieces.append(sbuf[b, h * hrow : h * hrow + half, :])
            pair = sbuf[b, h * hrow + half : (h + 1) * hrow, 0:half]
            cols.append(to_col(jnp.where(is0, pair[0:1], pair[1:2])))
        s = jnp.concatenate(pieces, axis=0)
        acol = jnp.concatenate(cols, axis=0)
        ss = split(s)
        st = split(s.T)
        total = jnp.zeros((rows, 1), F32)
        moved = jnp.zeros((rows, feats), F32)
        for j in range(nx):
            at = slice(j * rows, (j + 1) * rows)
            m = (mhi[at, :], mlo[at, :])
            g = dot3(ss, m, ((1,), (1,)))
            w = jnp.exp2(g * (2.0 * scale / feats) + acol + brow[0:1, at])
            total = total + jnp.sum(w, axis=1, keepdims=True)
            csum[0:1, at] += jnp.sum(w, axis=0, keepdims=True)
            ww = split(w)
            moved = moved + dot3(ww, m, ((1,), (0,)))
            gmt[:, at] += dot3(st, ww, ((1,), (0,)))
        part[b] = total * s - moved

    def step(s, carry):
        @pl.when(jnp.logical_and(s >= 1, s <= last))
        def _():
            b = z - s

            @pl.when(b >= 0)
            def _():
                zr_copy(s - 1, b).wait_recv()

                @pl.when(jnp.logical_and(has_right, s < last))
                def _():
                    zr_copy(s, b).start()

                sib_copy(b, mine).start()

            c = z + s

            @pl.when(c <= last)
            def _():
                zl_copy(s - 1, c).wait_recv()

                @pl.when(jnp.logical_and(has_left, s < last))
                def _():
                    zl_copy(s, c).start()

                sib_copy(c, mine).start()

        @pl.when(s == 0)
        def _():
            pl.when(has_right)(lambda: zr_copy(0, z).start())
            pl.when(has_left)(lambda: zl_copy(0, z).start())

        @pl.when(jnp.logical_and(fed, s == wait_m))
        def _():
            ref = mbuf.at[x]
            rdma(ref, ref, tm_s, tm_r, before).wait_recv()
            for k in range(nx - 1):
                mx_copy(k).start()

        pl.when(jnp.logical_and(active, s == first))(prepare)

        n = s - first

        @pl.when(jnp.logical_and(n >= 0, n < nz))
        def _():
            b = order(n)

            @pl.when(b != z)
            def _():
                sib_copy(b, other).wait_recv()

            @pl.when(jnp.logical_and(b == z, is0))
            def _():
                own_copy(1).wait_recv()

            pl.when(active)(lambda: tile(b))

            @pl.when(jnp.logical_not(active))
            def _():
                part[b] = jnp.zeros((rows, feats), F32)

            pe_copy(b, other_rows).start()

        return carry

    lax.fori_loop(0, 2 * nz + 1, step, 0)

    def gm_copy(k):
        j = lax.rem(x + 1 + k, nx)
        return rdma(gm.at[j], gm_in.at[k], gm_s.at[k], gm_r.at[k], xs[k])

    @pl.when(active)
    def _():
        for j in range(nx):
            at = slice(j * rows, (j + 1) * rows)
            ccol = to_col(csum[0:1, at])
            g = gmt[:, at].T
            for h in range(2):
                lo = h * half
                gm[j, lo : lo + half, :] = (
                    ccol[lo : lo + half] * mbuf[j, h * hrow : h * hrow + half, :] - g[lo : lo + half]
                )
        for k in range(nx - 1):
            gm_copy(k).start()

    def cr_copy(b):
        return rdma(right_sum.at[b], right_sum.at[b], cr_s.at[b], cr_r.at[b], zright)

    def cl_copy(b):
        return rdma(left_sum.at[b], left_sum.at[b], cl_s.at[b], cl_r.at[b], zleft)

    for b in range(nz):
        pe_copy(b, mine_rows).wait_recv()

    def chain(s, carry):
        @pl.when(jnp.logical_and(has_right, s >= z))
        def _():
            b = last - s + z

            @pl.when(has_left)
            def _():
                cr_copy(b).wait_recv()
                right_sum[b] = right_sum[b] + part[b, mine_rows, :] + sib_part[b]

            @pl.when(jnp.logical_not(has_left))
            def _():
                right_sum[b] = part[b, mine_rows, :] + sib_part[b]

            cr_copy(b).start()

        @pl.when(jnp.logical_and(has_left, s >= last - z))
        def _():
            b = s + z - last

            @pl.when(has_right)
            def _():
                cl_copy(b).wait_recv()
                left_sum[b] = left_sum[b] + part[b, mine_rows, :] + sib_part[b]

            @pl.when(jnp.logical_not(has_right))
            def _():
                left_sum[b] = part[b, mine_rows, :] + sib_part[b]

            cl_copy(b).start()

        @pl.when(jnp.logical_and(active, s == 1))
        def _():
            total = gm[x]
            for k in range(nx - 1):
                gm_copy(k).wait_recv()
                total = total + gm_in[k]
            gm[x] = total

            @pl.when(is1)
            def _():
                rdma(gm.at[x], gtm_in, gt_s, gt_r, after).start()

        return carry

    lax.fori_loop(0, last, chain, 0)

    mine_sum = part[z, mine_rows, :] + sib_part[z]
    fin[0] = mine_sum

    @pl.when(has_left)
    def _():
        cr_copy(z).wait_recv()
        fin[0] = fin[0] + right_sum[z]

    @pl.when(has_right)
    def _():
        cl_copy(z).wait_recv()
        fin[0] = fin[0] + left_sum[z]

    fin_copy = rdma(fin.at[0], fin.at[1], fin_s, fin_r, sib)
    gt_copy = rdma(gm.at[x], gtm_in, gt_s, gt_r, after)

    @pl.when(is0)
    def _():
        fin_copy.start()
        out_ref[...] = gm[x]

        @pl.when(feeds)
        def _():
            gt_copy.wait_recv()
            out_ref[...] = out_ref[...] + gtm_in[...]

    @pl.when(is1)
    def _():
        out_ref[half:, :] = fin[0]
        fin_copy.wait_recv()
        out_ref[0:half, :] = fin[1]

    @pl.when(is1)
    def _():
        own_copy(0).wait_send()
        own_copy(1).wait_send()

    pl.when(is0)(lambda: fin_copy.wait_send())
    pl.when(feeds)(lambda: tm_copy().wait_send())
    pl.when(fed)(lambda: gt_copy.wait_send())

    @pl.when(active)
    def _():
        for k in range(nx - 1):
            mx_copy(k).wait_send()
            gm_copy(k).wait_send()

    def drain(b, carry):
        pe_copy(b, other_rows).wait_send()

        @pl.when(b != z)
        def _():
            sib_copy(b, mine).wait_send()

        @pl.when(jnp.logical_and(has_right, b <= z))
        def _():
            zr_copy(z - b, b).wait_send()

        @pl.when(jnp.logical_and(has_left, b >= z))
        def _():
            zl_copy(b - z, b).wait_send()

        pl.when(jnp.logical_and(has_right, b > z))(lambda: cr_copy(b).wait_send())
        pl.when(jnp.logical_and(has_left, b < z))(lambda: cl_copy(b).wait_send())
        return carry

    lax.fori_loop(0, nz, drain, 0)


def local(dims, particles, source_pots, target_pots):
    times, nx, nz, rows, feats = dims
    half = rows // 2
    dma = pltpu.SemaphoreType.DMA
    scratch = [
        pltpu.VMEM((nz, rows + 16, feats), F32),
        pltpu.VMEM((nx, rows + 16, feats), F32),
        pltpu.VMEM((nx * rows, feats), BF16),
        pltpu.VMEM((nx * rows, feats), BF16),
        pltpu.VMEM((8, nx * rows), F32),
        pltpu.VMEM((nz, rows, feats), F32),
        pltpu.VMEM((nz, half, feats), F32),
        pltpu.VMEM((nz, half, feats), F32),
        pltpu.VMEM((nz, half, feats), F32),
        pltpu.VMEM((feats, nx * rows), F32),
        pltpu.VMEM((8, nx * rows), F32),
        pltpu.VMEM((nx, rows, feats), F32),
        pltpu.VMEM((nx - 1, rows, feats), F32),
        pltpu.VMEM((rows, feats), F32),
        pltpu.VMEM((2, half, feats), F32),
    ]
    for count in (nz, nz, nz, 2, 0, nx - 1, nz, nz, nz, nx - 1, 0, 0):
        kind = dma((count,)) if count else dma
        scratch += [kind, kind]
    out = pl.pallas_call(
        functools.partial(kernel, dims),
        out_shape=jax.ShapeDtypeStruct((rows, feats), F32),
        in_specs=[pl.BlockSpec(memory_space=pltpu.VMEM)] * 3,
        out_specs=pl.BlockSpec(memory_space=pltpu.VMEM),
        scratch_shapes=scratch,
        compiler_params=pltpu.CompilerParams(
            collective_id=0, has_side_effects=True, vmem_limit_bytes=56 * 2**20
        ),
    )(particles[0], source_pots, target_pots)
    return out[None]


def solution(mesh):
    times, nx, nz = mesh.shape["tm"], mesh.shape["row"], mesh.shape["col"]

    def program(particles, source_pots, target_pots):
        rows = particles.shape[1] // (nx * nz)
        dims = (times, nx, nz, rows, particles.shape[2])
        return jax.shard_map(
            functools.partial(local, dims),
            mesh=mesh,
            in_specs=(P("tm", ("row", "col"), None), P("tm", ("row", "col")), P("tm", ("row", "col"))),
            out_specs=P("tm", ("row", "col"), None),
            check_vma=False,
        )(particles, source_pots, target_pots)

    return program
```

time: 384 us -> 114 us (0.30)
  the two profiles are of different devices: /device:TPU:448 before, /device:TPU:57 now
where the time goes in v1:
time: 114 us
  Pallas kernels  112 us (98%)
  local copies, waits for them, and re-layouts  1.67 us (1%)
    pallas_call x1, Pallas kernels, local(): pl.pallas_call(functools.partial(kernel, dims), out_shape=jax.ShapeDtypeS...  112 us

profile of v1, /device:TPU:57, one launch (start us, length us, event | category | flops | bytes accessed | tf_op | source)
XLA Modules:
  0.0 113.9 jit_solution(14812431907124495800)
XLA Ops:
  0.0 112.2 %shard_map.37 = f32[256,256]{1,0:T(8,128)} custom-call(f32[256,256]{1,0:T(8,128)} %bitcast.3, f32[1,256]{1,0:T(1,128)} %spot_ref.1, f32[1,256]{1,0:T(1,128)} %tpot_ref.1), custom_call_target="tpu_custom_call" | custom-call | tf_op jit(solution)/shard_map/pallas_call | solution.py:478
  112.2 1.7 %copy.5 = f32[1,256,256]{2,1,0:T(8,128)} copy(f32[1,256,256]{2,1,0:T(8,128)} %bitcast.2) | data formatting | bytes 524288

commit v2 on v0

v2 whole, which is shorter than its diff:
```python
import functools
import math

import jax
import jax.numpy as jnp
from jax import lax
from jax.experimental import pallas as pl
from jax.experimental.pallas import tpu as pltpu
from jax.sharding import PartitionSpec as P

EPS = 0.1
MESH = pl.DeviceIdType.MESH
F32 = jnp.float32
BF16 = jnp.bfloat16


def split(x):
    hi = x.astype(BF16)
    return hi, (x - hi.astype(F32)).astype(BF16)


def dot(a, b, dims):
    return lax.dot_general(a, b, (dims, ((), ())), preferred_element_type=F32)


def dot3(a, b, dims):
    return dot(a[0], b[0], dims) + dot(a[0], b[1], dims) + dot(a[1], b[0], dims)


def eye(n):
    return lax.broadcasted_iota(jnp.int32, (n, n), 0) == lax.broadcasted_iota(jnp.int32, (n, n), 1)


def to_row(col):
    n = col.shape[0]
    return jnp.sum(jnp.where(eye(n), col, 0.0), axis=0, keepdims=True)


def to_col(row):
    n = row.shape[1]
    return jnp.sum(jnp.where(eye(n), row, 0.0), axis=1, keepdims=True)


BUFS = (
    "sbuf", "mbuf", "mhi", "mlo", "brow", "part", "sib_part", "rsum", "lsum", "gmt", "csum", "gm",
    "gx_in", "gmid", "gtm_in", "fin", "relay", "back", "shi", "slo", "thi", "tlo", "acol",
)
SEMS = (
    "own", "zr", "zl", "sib", "tm", "mx", "pe", "cr", "cl", "gx", "gt", "fi",
    "fx", "bx",
)
CH = 2


def kernel(dims, pts_ref, spot_ref, tpot_ref, out_ref, *scratch):
    times, nx, nz, rows, feats = dims
    half = rows // 2
    hrow = half + 8
    piece = half // CH
    last = nz - 1
    mid = times // 2
    spread = mid // 2
    population = rows * nx * nz
    scale = math.log2(math.e) / EPS
    v = dict(zip(BUFS, scratch))
    sems = {name: scratch[len(BUFS) + 2 * i : len(BUFS) + 2 * i + 2] for i, name in enumerate(SEMS)}
    sbuf, mbuf, part, gm, fin = v["sbuf"], v["mbuf"], v["part"], v["gm"], v["fin"]
    mhi, mlo, brow, gmt, csum = v["mhi"], v["mlo"], v["brow"], v["gmt"], v["csum"]
    gx_in = v["gx_in"]

    tm, x, z = lax.axis_index("tm"), lax.axis_index("row"), lax.axis_index("col")
    core = lax.rem(tm, 2)
    is0, is1 = core == 0, core == 1
    active = tm < times - 1
    cross = tm == mid - 1
    crossed = tm == mid
    fed = jnp.logical_and(jnp.logical_and(is1, active), jnp.logical_not(cross))
    feeds = jnp.logical_and(jnp.logical_and(is0, tm > 0), jnp.logical_not(crossed))
    has_left, has_right = z > 0, z < last
    sib = (tm + 1 - 2 * core, x, z)
    zright, zleft = (tm, x, jnp.minimum(z + 1, last)), (tm, x, jnp.maximum(z - 1, 0))
    before, after = (jnp.maximum(tm - 1, 0), x, z), (jnp.minimum(tm + 1, times - 1), x, z)
    x1, x2, x3 = lax.rem(x + 1, nx), lax.rem(x + 2, nx), lax.rem(x + 3, nx)
    xright, xleft = (tm, x1, z), (tm, x3, z)

    def at_time(t):
        return (t, x, z)

    def rdma(src, dst, name, to, k=None):
        s, r = sems[name]
        if k is not None:
            s, r = s.at[k], r.at[k]
        return pltpu.make_async_remote_copy(
            src_ref=src, dst_ref=dst, send_sem=s, recv_sem=r, device_id=to, device_id_type=MESH
        )

    barrier = pltpu.get_barrier_semaphore()

    def greet(to):
        pl.semaphore_signal(barrier, inc=1, device_id=to, device_id_type=MESH)

    for to in (sib, xright, xleft):
        greet(to)
    pl.when(has_left)(lambda: greet(zleft))
    pl.when(has_right)(lambda: greet(zright))
    pl.when(feeds)(lambda: greet(before))
    pl.when(fed)(lambda: greet(after))
    partners = 3 + has_left.astype(jnp.int32) + has_right.astype(jnp.int32)
    partners = partners + feeds.astype(jnp.int32) + fed.astype(jnp.int32)
    far = [mid + 2 * p for p in range(spread)]
    near = [2 * p for p in range(spread)]
    for p in range(spread):
        pl.when(cross)(lambda: greet(at_time(near[p])))
        pl.when(tm == near[p])(lambda: greet(at_time(far[p] if p else mid)))
        if p:
            pl.when(tm == far[p])(lambda: greet(at_time(mid)))

    relaying = jnp.logical_and(is0, jnp.logical_not(crossed))
    partners = partners + jnp.where(crossed, spread, relaying.astype(jnp.int32))

    pts = pts_ref[...]
    norm = to_row(jnp.sum(pts * pts, axis=1, keepdims=True)) * (scale / feats)
    trow = tpot_ref[...] * scale - norm
    srow = spot_ref[...] * scale - norm - math.log2(population)

    def put(buf, b):
        for i in range(2):
            buf[b, i * hrow : i * hrow + half, :] = pts[i * half : (i + 1) * half]
            pair = jnp.concatenate(
                [trow[:, i * half : (i + 1) * half], srow[:, i * half : (i + 1) * half], jnp.zeros((6, half), F32)], axis=0
            )
            buf[b, i * hrow + half : (i + 1) * hrow, :] = jnp.concatenate(
                [pair, jnp.zeros((8, feats - half), F32)], axis=1
            )

    pl.when(is0)(lambda: put(mbuf, x))
    pl.when(is1)(lambda: put(sbuf, z))

    pl.semaphore_wait(barrier, partners)

    mine = pl.ds(pl.multiple_of(core * hrow, 8), hrow)
    other = pl.ds(pl.multiple_of((1 - core) * hrow, 8), hrow)
    mine_rows = pl.ds(pl.multiple_of(core * half, 8), half)
    other_rows = pl.ds(pl.multiple_of((1 - core) * half, 8), half)

    def chunk(c):
        size = piece + (8 if c == CH - 1 else 0)
        return pl.ds(pl.multiple_of(core * hrow + c * piece, 8), size)

    def own_copy(i):
        ref = sbuf.at[z, pl.ds(i * hrow, hrow)]
        return rdma(ref, ref, "own", sib, i)

    def tm_copy():
        return rdma(mbuf.at[x], mbuf.at[x], "tm", before)

    h0, h1 = pl.ds(0, hrow), pl.ds(hrow, hrow)

    def mx_send(k):
        if k < 2:
            ref = mbuf.at[x]
        else:
            ref = mbuf.at[x3, h0] if k == 2 else mbuf.at[x1, h1]
        return rdma(ref, ref, "mx", xright if k % 2 == 0 else xleft, k)

    def mx_arrival(k):
        if k < 2:
            ref = mbuf.at[x3] if k == 0 else mbuf.at[x1]
        else:
            ref = mbuf.at[x2, h0] if k == 2 else mbuf.at[x2, h1]
        return rdma(ref, ref, "mx", xright, k)

    pieces = []
    for i in range(2):
        at = i * hrow
        pieces += [(at, half // 2), (at + half // 2, half // 2 + 8)]

    def fx_first(p):
        at, size = pieces[p]
        dst = v["relay"].at[pl.ds(0, size)]
        return rdma(mbuf.at[x, pl.ds(at, size)], dst, "fx", at_time(far[p] if p else near[p]), p)

    def fx_second(p):
        ref = v["relay"].at[pl.ds(0, pieces[p][1])]
        return rdma(ref, ref, "fx", at_time(near[p]), p)

    def fx_third(p):
        at, size = pieces[p]
        src = v["relay"].at[pl.ds(0, size)]
        return rdma(src, mbuf.at[x, pl.ds(at, size)], "fx", at_time(mid - 1), p)

    quarter = rows // spread

    def bx_first(p):
        return rdma(gm.at[x, pl.ds(p * quarter, quarter)], v["back"], "bx", at_time(near[p]), p)

    def bx_second(p):
        dst = v["back"] if p else v["gtm_in"].at[pl.ds(0, quarter)]
        return rdma(v["back"], dst, "bx", at_time(far[p] if p else mid), p)

    def bx_third(p):
        return rdma(v["back"], v["gtm_in"].at[pl.ds(p * quarter, quarter)], "bx", at_time(mid), p)

    @pl.when(is1)
    def _():
        own_copy(0).start()
        own_copy(1).start()

    @pl.when(is0)
    def _():
        pl.when(feeds)(lambda: tm_copy().start())

        @pl.when(crossed)
        def _():
            for p in range(spread):
                fx_first(p).start()

        mx_send(0).start()
        mx_send(1).start()
        own_copy(0).wait_recv()

    def zr_copy(s, c, b):
        ref = sbuf.at[b, chunk(c)]
        return rdma(ref, ref, "zr", zright, s * CH + c)

    def zl_copy(s, c, b):
        ref = sbuf.at[b, chunk(c)]
        return rdma(ref, ref, "zl", zleft, s * CH + c)

    def sib_copy(b, window):
        ref = sbuf.at[b, window]
        return rdma(ref, ref, "sib", sib, b)

    wait_m = jnp.where(cross, nz, 2)
    mx_step = jnp.where(cross, nz + 1, jnp.where(is0, 2, 4))
    first = jnp.where(cross, nz + 2, jnp.where(is0, 4, 6))
    late = jnp.logical_or(cross, tm == mid - 2)
    chain_at = jnp.where(late, nz + 3, nz + 1)
    ahead = jnp.maximum(nz - first, 0)

    def order(n):
        k = lax.rem(n + nz - ahead, nz)
        low = jnp.minimum(z, last - z)
        single = last - 2 * low
        d = (k - single) // 2
        b = jnp.where(k < single, last - k, jnp.where(lax.rem(k - single, 2) == 0, 2 * low - d, d))
        return jnp.where(z < nz - nz // 2, b, last - b)

    def pe_copy(b, window):
        return rdma(part.at[b, window], v["sib_part"].at[b], "pe", sib, b)

    def prepare():
        mx_arrival(2).wait_recv()
        mx_arrival(3).wait_recv()
        for j in range(nx):
            for i in range(2):
                at = j * rows + i * half
                hi, lo = split(mbuf[j, i * hrow : i * hrow + half, :])
                mhi[at : at + half, :] = hi
                mlo[at : at + half, :] = lo
                pair = mbuf[j, i * hrow + half : (i + 1) * hrow, 0:half]
                brow[0:1, at : at + half] = jnp.where(is0, pair[1:2], pair[0:1])

    def tile_open(b):
        for i in range(2):
            at = slice(i * half, (i + 1) * half)
            s = sbuf[b, i * hrow : i * hrow + half, :]
            hi, lo = split(s)
            v["shi"][at, :] = hi
            v["slo"][at, :] = lo
            hi, lo = split(s.T)
            v["thi"][:, at] = hi
            v["tlo"][:, at] = lo
            pair = sbuf[b, i * hrow + half : (i + 1) * hrow, 0:half]
            v["acol"][at, :] = jnp.broadcast_to(to_col(jnp.where(is0, pair[0:1], pair[1:2])), (half, half))

    def tile_part(b, c):
        width = nx * rows // CH
        at = slice(c * width, (c + 1) * width)
        m = (mhi[at, :], mlo[at, :])
        g = dot3((v["shi"][...], v["slo"][...]), m, ((1,), (1,)))
        w = jnp.exp2(g * (2.0 * scale / feats) + v["acol"][:, 0:1] + brow[0:1, at])
        total = jnp.sum(w, axis=1, keepdims=True)
        csum[0:1, at] += jnp.sum(w, axis=0, keepdims=True)
        ww = split(w)
        moved = dot3(ww, m, ((1,), (0,)))
        gmt[:, at] += dot3((v["thi"][...], v["tlo"][...]), ww, ((1,), (0,)))
        for i in range(2):
            r = slice(i * half, (i + 1) * half)
            term = total[r] * sbuf[b, i * hrow : i * hrow + half, :] - moved[r]
            part[b, r, :] = term if c == 0 else part[b, r, :] + term

    gmt[...] = jnp.zeros_like(gmt)
    csum[...] = jnp.zeros_like(csum)

    g0, g1 = pl.ds(0, half), pl.ds(half, half)

    def gx_copy(k):
        src, dst = [
            (gm.at[x2, g0], v["gmid"].at[0]),
            (gm.at[x2, g1], v["gmid"].at[1]),
            (gm.at[x1, g1], gx_in.at[0, g1]),
            (gm.at[x3, g0], gx_in.at[1, g0]),
            (gm.at[x1, g0], gx_in.at[0, g0]),
            (gm.at[x3, g1], gx_in.at[1, g1]),
        ][k]
        return rdma(src, dst, "gx", xright if k % 2 == 0 else xleft, k)

    def finish_m(j):
        at = pl.ds(pl.multiple_of(j * rows, rows), rows)
        ccol = to_col(csum[0:1, at])
        g = gmt[:, at].T
        for i in range(2):
            lo = i * half
            gm[j, lo : lo + half, :] = ccol[lo : lo + half] * mbuf[j, i * hrow : i * hrow + half, :] - g[lo : lo + half]

    def gt_copy():
        return rdma(gm.at[x], v["gtm_in"], "gt", after)

    def cr_copy(b, c):
        ref = v["rsum"].at[b, pl.ds(c * piece, piece)]
        return rdma(ref, ref, "cr", zright, b * CH + c)

    def cl_copy(b, c):
        ref = v["lsum"].at[b, pl.ds(c * piece, piece)]
        return rdma(ref, ref, "cl", zleft, b * CH + c)

    def link(b, c, copy, total, begun):
        r = pl.ds(c * piece, piece)
        mine_r = pl.ds(pl.multiple_of(core * half + c * piece, 8), piece)

        @pl.when(begun)
        def _():
            copy(b, c).wait_recv()
            total[b, r, :] = total[b, r, :] + part[b, mine_r, :] + v["sib_part"][b, r, :]

        @pl.when(jnp.logical_not(begun))
        def _():
            total[b, r, :] = part[b, mine_r, :] + v["sib_part"][b, r, :]

        copy(b, c).start()

    def step(s, carry):
        n = s - first
        has_tile = jnp.logical_and(n >= 0, n < nz)
        b = order(jnp.clip(n, 0, last))
        computes = jnp.logical_and(has_tile, active)
        relays = jnp.logical_and(s >= 1, s <= last)
        from_left = jnp.logical_and(relays, z - s >= 0)
        from_right = jnp.logical_and(relays, z + s <= last)

        for p in range(1, spread):

            @pl.when(jnp.logical_and(s == 1, tm == far[p]))
            def _():
                fx_second(p).wait_recv()
                fx_second(p).start()

        for p in range(spread):

            @pl.when(jnp.logical_and(s == nz - 2, tm == near[p]))
            def _():
                fx_second(p).wait_recv()
                fx_third(p).start()

        @pl.when(s == wait_m)
        def _():
            @pl.when(fed)
            def _():
                tm_copy().wait_recv()

            @pl.when(cross)
            def _():
                for p in range(spread):
                    at, size = pieces[p]
                    ref = mbuf.at[x, pl.ds(at, size)]
                    rdma(ref, ref, "fx", at_time(mid - 1), p).wait_recv()

            @pl.when(jnp.logical_or(fed, cross))
            def _():
                mx_send(0).start()
                mx_send(1).start()

        @pl.when(jnp.logical_and(active, s == mx_step))
        def _():
            mx_arrival(0).wait_recv()
            mx_send(2).start()
            mx_arrival(1).wait_recv()
            mx_send(3).start()

        pl.when(jnp.logical_and(active, s == first))(prepare)

        @pl.when(has_tile)
        def _():
            @pl.when(b != z)
            def _():
                sib_copy(b, other).wait_recv()

            @pl.when(jnp.logical_and(b == z, is0))
            def _():
                own_copy(1).wait_recv()

        for c in range(CH):

            @pl.when(s == 0)
            def _():
                pl.when(has_right)(lambda: zr_copy(0, c, z).start())
                pl.when(has_left)(lambda: zl_copy(0, c, z).start())

            @pl.when(from_left)
            def _():
                zr_copy(s - 1, c, z - s).wait_recv()

                @pl.when(jnp.logical_and(has_right, s < last))
                def _():
                    zr_copy(s, c, z - s).start()

                if c == CH - 1:
                    sib_copy(z - s, mine).start()

            @pl.when(from_right)
            def _():
                zl_copy(s - 1, c, z + s).wait_recv()

                @pl.when(jnp.logical_and(has_left, s < last))
                def _():
                    zl_copy(s, c, z + s).start()

                if c == CH - 1:
                    sib_copy(z + s, mine).start()

            @pl.when(computes)
            def _():
                if c == 0:
                    tile_open(b)
                tile_part(b, c)

        @pl.when(has_tile)
        def _():
            @pl.when(jnp.logical_not(active))
            def _():
                part[b] = jnp.zeros((rows, feats), F32)

            pe_copy(b, other_rows).start()

        cs = s - chain_at
        linked = jnp.logical_and(cs >= 0, cs < last)
        goes_right = jnp.logical_and(linked, jnp.logical_and(has_right, cs >= z))
        goes_left = jnp.logical_and(linked, jnp.logical_and(has_left, cs >= last - z))
        br, bl = last - cs + z, cs + z - last
        pl.when(goes_right)(lambda: pe_copy(br, mine_rows).wait_recv())
        pl.when(goes_left)(lambda: pe_copy(bl, mine_rows).wait_recv())
        for c in range(CH):
            pl.when(goes_right)(lambda: link(br, c, cr_copy, v["rsum"], has_left))
            pl.when(goes_left)(lambda: link(bl, c, cl_copy, v["lsum"], has_right))

        done = s - first - nz

        @pl.when(jnp.logical_and(active, done == 0))
        def _():
            finish_m(x2)
            gx_copy(0).start()
            gx_copy(1).start()
            finish_m(x1)
            gx_copy(2).start()
            finish_m(x3)
            gx_copy(3).start()
            finish_m(x)

        @pl.when(jnp.logical_and(active, done == 2))
        def _():
            gx_copy(0).wait_recv()
            gm[x1, g0, :] = gm[x1, g0, :] + v["gmid"][0]
            gx_copy(4).start()
            gx_copy(1).wait_recv()
            gm[x3, g1, :] = gm[x3, g1, :] + v["gmid"][1]
            gx_copy(5).start()

        @pl.when(jnp.logical_and(active, done == 4))
        def _():
            for k in range(2, 6):
                gx_copy(k).wait_recv()
            gm[x] = gm[x] + gx_in[0] + gx_in[1]
            pl.when(fed)(lambda: gt_copy().start())

            @pl.when(cross)
            def _():
                for p in range(spread):
                    bx_first(p).start()

        return carry

    lax.fori_loop(0, 2 * nz + 7, step, 0)

    pe_copy(z, mine_rows).wait_recv()
    fin[0] = part[z, mine_rows, :] + v["sib_part"][z]
    for c in range(CH):
        r = pl.ds(c * piece, piece)

        @pl.when(has_left)
        def _():
            cr_copy(z, c).wait_recv()
            fin[0, r, :] = fin[0, r, :] + v["rsum"][z, r, :]

        @pl.when(has_right)
        def _():
            cl_copy(z, c).wait_recv()
            fin[0, r, :] = fin[0, r, :] + v["lsum"][z, r, :]

    fin_copy = rdma(fin.at[0], fin.at[1], "fi", sib)

    @pl.when(is0)
    def _():
        fin_copy.start()
        out_ref[...] = gm[x]

        @pl.when(feeds)
        def _():
            gt_copy().wait_recv()
            out_ref[...] = out_ref[...] + v["gtm_in"][...]

    for p in range(spread):

        @pl.when(tm == near[p])
        def _():
            bx_second(p).wait_recv() if p else bx_first(p).wait_recv()
            bx_second(p).start()

    for p in range(1, spread):

        @pl.when(tm == far[p])
        def _():
            bx_second(p).wait_recv()
            bx_third(p).start()

    @pl.when(crossed)
    def _():
        for p in range(spread):
            bx_third(p).wait_recv()
        out_ref[...] = out_ref[...] + v["gtm_in"][...]

    @pl.when(is1)
    def _():
        out_ref[half:, :] = fin[0]
        fin_copy.wait_recv()
        out_ref[0:half, :] = fin[1]

    @pl.when(is1)
    def _():
        own_copy(0).wait_send()
        own_copy(1).wait_send()

    pl.when(is0)(lambda: fin_copy.wait_send())
    pl.when(feeds)(lambda: tm_copy().wait_send())
    pl.when(fed)(lambda: gt_copy().wait_send())
    for p in range(spread):

        @pl.when(crossed)
        def _():
            fx_first(p).wait_send()

        @pl.when(cross)
        def _():
            bx_first(p).wait_send()

        @pl.when(tm == near[p])
        def _():
            fx_third(p).wait_send()
            bx_second(p).wait_send()

        if p:

            @pl.when(tm == far[p])
            def _():
                fx_second(p).wait_send()
                bx_third(p).wait_send()

    @pl.when(active)
    def _():
        for k in range(4):
            mx_send(k).wait_send()
        for k in range(6):
            gx_copy(k).wait_send()

    def drain(b, carry):
        pe_copy(b, other_rows).wait_send()

        @pl.when(b != z)
        def _():
            sib_copy(b, mine).wait_send()

        for c in range(CH):
            pl.when(jnp.logical_and(has_right, b <= z))(lambda: zr_copy(z - b, c, b).wait_send())
            pl.when(jnp.logical_and(has_left, b >= z))(lambda: zl_copy(b - z, c, b).wait_send())
            pl.when(jnp.logical_and(has_right, b > z))(lambda: cr_copy(b, c).wait_send())
            pl.when(jnp.logical_and(has_left, b < z))(lambda: cl_copy(b, c).wait_send())
        return carry

    lax.fori_loop(0, nz, drain, 0)


def local(dims, particles, source_pots, target_pots):
    times, nx, nz, rows, feats = dims
    half = rows // 2
    spread = times // 4
    dma = pltpu.SemaphoreType.DMA
    shapes = [
        ((nz, rows + 16, feats), F32),
        ((nx, rows + 16, feats), F32),
        ((nx * rows, feats), BF16),
        ((nx * rows, feats), BF16),
        ((8, nx * rows), F32),
        ((nz, rows, feats), F32),
        ((nz, half, feats), F32),
        ((nz, half, feats), F32),
        ((nz, half, feats), F32),
        ((feats, nx * rows), F32),
        ((8, nx * rows), F32),
        ((nx, rows, feats), F32),
        ((2, rows, feats), F32),
        ((2, half, feats), F32),
        ((rows, feats), F32),
        ((2, half, feats), F32),
        ((half // 2 + 8, feats), F32),
        ((rows // spread, feats), F32),
        ((rows, feats), BF16),
        ((rows, feats), BF16),
        ((feats, rows), BF16),
        ((feats, rows), BF16),
        ((rows, half), F32),
    ]
    scratch = [pltpu.VMEM(shape, kind) for shape, kind in shapes]
    line = nz * CH
    for count in (2, line, line, nz, 0, 4, nz, line, line, 6, 0, 0, spread, spread):
        kind = dma((count,)) if count else dma
        scratch += [kind, kind]
    out = pl.pallas_call(
        functools.partial(kernel, dims),
        out_shape=jax.ShapeDtypeStruct((rows, feats), F32),
        in_specs=[pl.BlockSpec(memory_space=pltpu.VMEM)] * 3,
        out_specs=pl.BlockSpec(memory_space=pltpu.VMEM),
        scratch_shapes=scratch,
        compiler_params=pltpu.CompilerParams(
            collective_id=0, has_side_effects=True, vmem_limit_bytes=56 * 2**20
        ),
    )(particles[0], source_pots, target_pots)
    return out[None]


def solution(mesh):
    times, nx, nz = mesh.shape["tm"], mesh.shape["row"], mesh.shape["col"]

    def program(particles, source_pots, target_pots):
        rows = particles.shape[1] // (nx * nz)
        dims = (times, nx, nz, rows, particles.shape[2])
        return jax.shard_map(
            functools.partial(local, dims),
            mesh=mesh,
            in_specs=(P("tm", ("row", "col"), None), P("tm", ("row", "col")), P("tm", ("row", "col"))),
            out_specs=P("tm", ("row", "col"), None),
            check_vma=False,
        )(particles, source_pots, target_pots)

    return program
```

time: 384 us -> 92.2 us (0.24)
  the two profiles are of different devices: /device:TPU:448 before, /device:TPU:352 now
where the time goes in v2:
time: 92.2 us; the launch traced here: 92.1 us
  Pallas kernels  90.4 us (98%)
  local copies, waits for them, and re-layouts  1.67 us (2%)
    pallas_call x1, Pallas kernels, local(): pl.pallas_call(functools.partial(kernel, dims), out_shape=jax.ShapeDtypeS...  90.4 us

profile of v2, /device:TPU:352, one launch (start us, length us, event | category | flops | bytes accessed | tf_op | source)
XLA Modules:
  0.0 92.1 jit_solution(8558496527343078372)
XLA Ops:
  0.0 90.4 %shard_map.37 = f32[256,256]{1,0:T(8,128)} custom-call(f32[256,256]{1,0:T(8,128)} %bitcast.3, f32[1,256]{1,0:T(1,128)} %spot_ref.1, f32[1,256]{1,0:T(1,128)} %tpot_ref.1), custom_call_target="tpu_custom_call" | custom-call | tf_op jit(solution)/shard_map/pallas_call | solution.py:637
  90.4 1.7 %copy.5 = f32[1,256,256]{2,1,0:T(8,128)} copy(f32[1,256,256]{2,1,0:T(8,128)} %bitcast.2) | data formatting | bytes 524288

commit v3 on v2

v3 whole, which is shorter than its diff:
```python
import functools
import math

import jax
import jax.numpy as jnp
from jax import lax
from jax.experimental import pallas as pl
from jax.experimental.pallas import tpu as pltpu
from jax.sharding import PartitionSpec as P

EPS = 0.1
MESH = pl.DeviceIdType.MESH
F32 = jnp.float32
BF16 = jnp.bfloat16


def split(x):
    hi = x.astype(BF16)
    return hi, (x - hi.astype(F32)).astype(BF16)


def dot(a, b, dims):
    return lax.dot_general(a, b, (dims, ((), ())), preferred_element_type=F32)


def dot3(a, b, dims):
    return dot(a[0], b[0], dims) + dot(a[0], b[1], dims) + dot(a[1], b[0], dims)


def eye(n):
    return lax.broadcasted_iota(jnp.int32, (n, n), 0) == lax.broadcasted_iota(jnp.int32, (n, n), 1)


def to_row(col):
    n = col.shape[0]
    return jnp.sum(jnp.where(eye(n), col, 0.0), axis=0, keepdims=True)


def to_col(row):
    n = row.shape[1]
    return jnp.sum(jnp.where(eye(n), row, 0.0), axis=1, keepdims=True)


BUFS = (
    "sbuf", "mbuf", "mhi", "mlo", "brow", "part", "sib_part", "rsum", "gmt", "csum", "gm",
    "gx_in", "gmid", "gtm_in", "fin", "relay", "back", "shi", "slo", "thi", "tlo", "acol",
)
SEMS = (
    "own", "zr", "sib", "tm", "mx", "pe", "cr", "gx", "gt", "fi",
    "fx", "bx",
)
CH = 4


def kernel(dims, pts_ref, spot_ref, tpot_ref, out_ref, *scratch):
    times, nx, nz, rows, feats = dims
    half = rows // 2
    hrow = half + 8
    piece = rows // CH
    last = nz - 1
    run = nz // 2
    mid = times // 2
    spread = mid // 2
    population = rows * nx * nz
    scale = math.log2(math.e) / EPS
    v = dict(zip(BUFS, scratch))
    sems = {name: scratch[len(BUFS) + 2 * i : len(BUFS) + 2 * i + 2] for i, name in enumerate(SEMS)}
    sbuf, mbuf, part, gm, fin = v["sbuf"], v["mbuf"], v["part"], v["gm"], v["fin"]
    mhi, mlo, brow, gmt, csum = v["mhi"], v["mlo"], v["brow"], v["gmt"], v["csum"]
    gx_in = v["gx_in"]

    tm, x, z = lax.axis_index("tm"), lax.axis_index("row"), lax.axis_index("col")
    core = lax.rem(tm, 2)
    is0, is1 = core == 0, core == 1
    active = tm < times - 1
    cross = tm == mid - 1
    crossed = tm == mid
    fed = jnp.logical_and(jnp.logical_and(is1, active), jnp.logical_not(cross))
    feeds = jnp.logical_and(jnp.logical_and(is0, tm > 0), jnp.logical_not(crossed))
    place = jnp.where(is0, z, last - z)
    has_prev, has_next = place > 0, place < last
    way = 1 - 2 * core
    forth = (tm, x, jnp.clip(z + way, 0, last))
    back_to = (tm, x, jnp.clip(z - way, 0, last))
    sib = (tm + 1 - 2 * core, x, z)
    before, after = (jnp.maximum(tm - 1, 0), x, z), (jnp.minimum(tm + 1, times - 1), x, z)
    x1, x2, x3 = lax.rem(x + 1, nx), lax.rem(x + 2, nx), lax.rem(x + 3, nx)
    xright, xleft = (tm, x1, z), (tm, x3, z)

    def at_time(t):
        return (t, x, z)

    def rdma(src, dst, name, to, k=None):
        s, r = sems[name]
        if k is not None:
            s, r = s.at[k], r.at[k]
        return pltpu.make_async_remote_copy(
            src_ref=src, dst_ref=dst, send_sem=s, recv_sem=r, device_id=to, device_id_type=MESH
        )

    barrier = pltpu.get_barrier_semaphore()

    def greet(to):
        pl.semaphore_signal(barrier, inc=1, device_id=to, device_id_type=MESH)

    for to in (sib, xright, xleft):
        greet(to)
    pl.when(has_prev)(lambda: greet(back_to))
    pl.when(feeds)(lambda: greet(before))
    pl.when(fed)(lambda: greet(after))
    partners = 3 + has_next.astype(jnp.int32)
    partners = partners + feeds.astype(jnp.int32) + fed.astype(jnp.int32)
    far = [mid + 2 * p for p in range(spread)]
    near = [2 * p for p in range(spread)]
    for p in range(spread):
        pl.when(cross)(lambda: greet(at_time(near[p])))
        pl.when(tm == near[p])(lambda: greet(at_time(far[p] if p else mid)))
        if p:
            pl.when(tm == far[p])(lambda: greet(at_time(mid)))

    relaying = jnp.logical_and(is0, jnp.logical_not(crossed))
    partners = partners + jnp.where(crossed, spread, relaying.astype(jnp.int32))

    pts = pts_ref[...]
    norm = to_row(jnp.sum(pts * pts, axis=1, keepdims=True)) * (scale / feats)
    trow = tpot_ref[...] * scale - norm
    srow = spot_ref[...] * scale - norm - math.log2(population)

    def put(buf, b):
        for i in range(2):
            buf[b, i * hrow : i * hrow + half, :] = pts[i * half : (i + 1) * half]
            pair = jnp.concatenate(
                [trow[:, i * half : (i + 1) * half], srow[:, i * half : (i + 1) * half], jnp.zeros((6, half), F32)], axis=0
            )
            buf[b, i * hrow + half : (i + 1) * hrow, :] = jnp.concatenate(
                [pair, jnp.zeros((8, feats - half), F32)], axis=1
            )

    pl.when(is0)(lambda: put(mbuf, x))
    pl.when(is1)(lambda: put(sbuf, z))

    pl.semaphore_wait(barrier, partners)

    def chunk(g, k):
        return pl.ds(pl.multiple_of(g * hrow + k * (half // 2), 8), half // 2 + 8 * k)

    def blk(i):
        return jnp.where(is0, i, last - i)

    def own_copy(i):
        ref = sbuf.at[z, pl.ds(i * hrow, hrow)]
        return rdma(ref, ref, "own", sib, i)

    def tm_copy():
        return rdma(mbuf.at[x], mbuf.at[x], "tm", before)

    h0, h1 = pl.ds(0, hrow), pl.ds(hrow, hrow)

    def mx_send(k):
        if k < 2:
            ref = mbuf.at[x]
        else:
            ref = mbuf.at[x3, h0] if k == 2 else mbuf.at[x1, h1]
        return rdma(ref, ref, "mx", xright if k % 2 == 0 else xleft, k)

    def mx_arrival(k):
        if k < 2:
            ref = mbuf.at[x3] if k == 0 else mbuf.at[x1]
        else:
            ref = mbuf.at[x2, h0] if k == 2 else mbuf.at[x2, h1]
        return rdma(ref, ref, "mx", xright, k)

    pieces = []
    for i in range(2):
        at = i * hrow
        pieces += [(at, half // 2), (at + half // 2, half // 2 + 8)]

    def fx_first(p):
        at, size = pieces[p]
        dst = v["relay"].at[pl.ds(0, size)]
        return rdma(mbuf.at[x, pl.ds(at, size)], dst, "fx", at_time(far[p] if p else near[p]), p)

    def fx_second(p):
        ref = v["relay"].at[pl.ds(0, pieces[p][1])]
        return rdma(ref, ref, "fx", at_time(near[p]), p)

    def fx_third(p):
        at, size = pieces[p]
        src = v["relay"].at[pl.ds(0, size)]
        return rdma(src, mbuf.at[x, pl.ds(at, size)], "fx", at_time(mid - 1), p)

    quarter = rows // spread

    def bx_first(p):
        return rdma(gm.at[x, pl.ds(p * quarter, quarter)], v["back"], "bx", at_time(near[p]), p)

    def bx_second(p):
        dst = v["back"] if p else v["gtm_in"].at[pl.ds(0, quarter)]
        return rdma(v["back"], dst, "bx", at_time(far[p] if p else mid), p)

    def bx_third(p):
        return rdma(v["back"], v["gtm_in"].at[pl.ds(p * quarter, quarter)], "bx", at_time(mid), p)

    def zr_part(s, g, k, b):
        ref = sbuf.at[b, chunk(g, k)]
        return rdma(ref, ref, "zr", forth, s * CH + 2 * g + k)

    def zr_copy(s, c, b):
        return zr_part(s, c // 2, c % 2, b)

    def sib_copy(b):
        return rdma(sbuf.at[b], sbuf.at[b], "sib", sib, b)

    @pl.when(is1)
    def _():
        own_copy(0).start()
        own_copy(1).start()
        for c in range(CH):
            pl.when(has_next)(lambda: zr_copy(0, c, z).start())

    @pl.when(is0)
    def _():
        pl.when(feeds)(lambda: tm_copy().start())

        @pl.when(crossed)
        def _():
            for p in range(spread):
                fx_first(p).start()

        mx_send(0).start()
        mx_send(1).start()
        for i in range(2):
            own_copy(i).wait_recv()
            for c in (2 * i, 2 * i + 1):
                pl.when(has_next)(lambda: zr_copy(0, c, z).start())

    chain_at = nz + 1
    near_at, far_at = run, 1
    wait_m = jnp.where(cross, run + 1, 1)
    mx_step = jnp.where(cross, run + 2, jnp.where(is0, 1, 3))
    first = jnp.where(cross, nz, jnp.where(is0, 3, 4))
    pace = jnp.where(cross, 2, 1)
    ahead = nz - first

    def order(n):
        k = jnp.where(n < ahead, last - n, n - ahead)
        low = jnp.minimum(z, last - z)
        single = last - 2 * low
        d = (k - single) // 2
        b = jnp.where(k < single, last - k, jnp.where(lax.rem(k - single, 2) == 0, 2 * low - d, d))
        return jnp.where(z < nz - nz // 2, b, last - b)

    def pe_copy(b):
        return rdma(part.at[b], v["sib_part"].at[b], "pe", sib, b)

    def prepare():
        mx_arrival(2).wait_recv()
        mx_arrival(3).wait_recv()
        for j in range(nx):
            for i in range(2):
                at = j * rows + i * half
                hi, lo = split(mbuf[j, i * hrow : i * hrow + half, :])
                mhi[at : at + half, :] = hi
                mlo[at : at + half, :] = lo
                pair = mbuf[j, i * hrow + half : (i + 1) * hrow, 0:half]
                brow[0:1, at : at + half] = jnp.where(is0, pair[1:2], pair[0:1])

    def tile_open(b):
        for i in range(2):
            at = slice(i * half, (i + 1) * half)
            s = sbuf[b, i * hrow : i * hrow + half, :]
            hi, lo = split(s)
            v["shi"][at, :] = hi
            v["slo"][at, :] = lo
            hi, lo = split(s.T)
            v["thi"][:, at] = hi
            v["tlo"][:, at] = lo
            pair = sbuf[b, i * hrow + half : (i + 1) * hrow, 0:half]
            v["acol"][at, :] = jnp.broadcast_to(to_col(jnp.where(is0, pair[0:1], pair[1:2])), (half, half))

    def tile_part(b, c):
        width = nx * rows // 2
        at = pl.ds(pl.multiple_of(c * width, width), width)
        m = (mhi[at, :], mlo[at, :])
        g = dot3((v["shi"][...], v["slo"][...]), m, ((1,), (1,)))
        w = jnp.exp2(g * (2.0 * scale / feats) + v["acol"][:, 0:1] + brow[0:1, at])
        total = jnp.sum(w, axis=1, keepdims=True)
        csum[0:1, at] += jnp.sum(w, axis=0, keepdims=True)
        ww = split(w)
        moved = dot3(ww, m, ((1,), (0,)))
        gmt[:, at] += dot3((v["thi"][...], v["tlo"][...]), ww, ((1,), (0,)))
        for i in range(2):
            r = slice(i * half, (i + 1) * half)
            part[b, r, :] = part[b, r, :] + (total[r] * sbuf[b, i * hrow : i * hrow + half, :] - moved[r])

    gmt[...] = jnp.zeros_like(gmt)
    csum[...] = jnp.zeros_like(csum)

    g0, g1 = pl.ds(0, half), pl.ds(half, half)

    def gx_copy(k):
        src, dst = [
            (gm.at[x2, g0], v["gmid"].at[0]),
            (gm.at[x2, g1], v["gmid"].at[1]),
            (gm.at[x1, g1], gx_in.at[0, g1]),
            (gm.at[x3, g0], gx_in.at[1, g0]),
            (gm.at[x1, g0], gx_in.at[0, g0]),
            (gm.at[x3, g1], gx_in.at[1, g1]),
        ][k]
        return rdma(src, dst, "gx", xright if k % 2 == 0 else xleft, k)

    def finish_m(j):
        at = pl.ds(pl.multiple_of(j * rows, rows), rows)
        ccol = to_col(csum[0:1, at])
        g = gmt[:, at].T
        for i in range(2):
            lo = i * half
            gm[j, lo : lo + half, :] = ccol[lo : lo + half] * mbuf[j, i * hrow : i * hrow + half, :] - g[lo : lo + half]

    def gt_copy():
        return rdma(gm.at[x], v["gtm_in"], "gt", after)

    def cr_copy(b, c):
        ref = v["rsum"].at[b, pl.ds(c * piece, piece)]
        return rdma(ref, ref, "cr", forth, b * CH + c)

    def fi_copy(c):
        r = pl.ds(c * piece, piece)
        return rdma(v["rsum"].at[z, r], fin.at[r], "fi", sib, c)

    def step(s, carry):
        @pl.when(jnp.logical_and(is0, jnp.logical_or(s == far_at, s == near_at)))
        def _():
            for p in range(1, spread):

                @pl.when(jnp.logical_and(s == far_at, tm == far[p]))
                def _():
                    fx_second(p).wait_recv()
                    fx_second(p).start()

            for p in range(spread):

                @pl.when(jnp.logical_and(s == near_at, tm == near[p]))
                def _():
                    fx_second(p).wait_recv()
                    fx_third(p).start()

        @pl.when(s <= first)
        def _():
            @pl.when(s == wait_m)
            def _():
                @pl.when(fed)
                def _():
                    tm_copy().wait_recv()

                @pl.when(cross)
                def _():
                    for p in range(spread):
                        at, size = pieces[p]
                        ref = mbuf.at[x, pl.ds(at, size)]
                        rdma(ref, ref, "fx", at_time(mid - 1), p).wait_recv()

                @pl.when(jnp.logical_or(fed, cross))
                def _():
                    mx_send(0).start()
                    mx_send(1).start()

            @pl.when(jnp.logical_and(active, s == mx_step))
            def _():
                mx_arrival(0).wait_recv()
                mx_send(2).start()
                mx_arrival(1).wait_recv()
                mx_send(3).start()

            pl.when(jnp.logical_and(active, s == first))(prepare)

        relays = jnp.logical_and(s <= last, s <= place)
        onward = jnp.logical_and(relays, jnp.logical_and(has_next, s < last))
        at = blk(place - s)

        def unit(u, carry):
            c = lax.rem(u, 2)
            n = (s - first) * pace + u // 2
            b = order(jnp.clip(n, 0, last))
            has_tile = jnp.logical_and(n >= 0, n < nz)

            @pl.when(jnp.logical_and(relays, u < 2))
            def _():
                for k in range(2):
                    zr_part(s - 1, u, k, at).wait_recv()
                    pl.when(onward)(lambda: zr_part(s, u, k, at).start())

            @pl.when(has_tile)
            def _():
                @pl.when(c == 0)
                def _():
                    pl.when(jnp.where(is0, b > z, b < z))(lambda: sib_copy(b).wait_recv())
                    part[b] = jnp.zeros((rows, feats), F32)
                    pl.when(active)(lambda: tile_open(b))

                pl.when(active)(lambda: tile_part(b, c))

                @pl.when(jnp.logical_and(c == 1, jnp.where(is0, b <= z, b > z)))
                def _():
                    pe_copy(b).start()

            return carry

        units = jnp.where(jnp.logical_or(s <= last, s < first + nz // pace), 2 * jnp.where(s < first, 1, pace), 0)
        lax.fori_loop(0, units, unit, 0)
        pl.when(relays)(lambda: sib_copy(at).start())

        cs = s - chain_at

        @pl.when(jnp.logical_and(jnp.logical_and(cs >= place, cs < last), has_next))
        def _():
            t = blk(last - cs + place)
            pe_copy(t).wait_recv()
            for c in range(CH):
                r = pl.ds(c * piece, piece)

                @pl.when(has_prev)
                def _():
                    cr_copy(t, c).wait_recv()
                    v["rsum"][t, r, :] = v["rsum"][t, r, :] + (part[t, r, :] + v["sib_part"][t, r, :])

                @pl.when(jnp.logical_not(has_prev))
                def _():
                    v["rsum"][t, r, :] = part[t, r, :] + v["sib_part"][t, r, :]

                cr_copy(t, c).start()

        done = s - first - nz // pace

        @pl.when(jnp.logical_and(active, done >= 0))
        def _():
            @pl.when(done == 0)
            def _():
                finish_m(x2)
                gx_copy(0).start()
                gx_copy(1).start()
                finish_m(x1)
                gx_copy(2).start()
                finish_m(x3)
                gx_copy(3).start()
                finish_m(x)

            @pl.when(done == 1)
            def _():
                gx_copy(0).wait_recv()
                gm[x1, g0, :] = gm[x1, g0, :] + v["gmid"][0]
                gx_copy(4).start()
                gx_copy(1).wait_recv()
                gm[x3, g1, :] = gm[x3, g1, :] + v["gmid"][1]
                gx_copy(5).start()

            @pl.when(done == 2)
            def _():
                for k in range(2, 6):
                    gx_copy(k).wait_recv()
                gm[x] = gm[x] + gx_in[0] + gx_in[1]
                pl.when(fed)(lambda: gt_copy().start())

                @pl.when(cross)
                def _():
                    for p in range(spread):
                        bx_first(p).start()

        return carry

    steps = jnp.maximum(first + nz // pace + 3, chain_at + last)
    lax.fori_loop(1, steps, step, 0)

    @pl.when(is0)
    def _():
        @pl.when(has_prev)
        def _():
            for c in range(CH):
                cr_copy(z, c).wait_recv()
                fi_copy(c).start()

        for p in range(spread):

            @pl.when(tm == near[p])
            def _():
                bx_first(p).wait_recv()
                bx_second(p).start()

        out_ref[...] = gm[x]

        @pl.when(feeds)
        def _():
            gt_copy().wait_recv()
            out_ref[...] = out_ref[...] + v["gtm_in"][...]

    for p in range(1, spread):

        @pl.when(tm == far[p])
        def _():
            bx_second(p).wait_recv()
            bx_third(p).start()

    @pl.when(crossed)
    def _():
        for p in range(spread):
            bx_third(p).wait_recv()
        out_ref[...] = out_ref[...] + v["gtm_in"][...]

    @pl.when(is1)
    def _():
        pe_copy(z).wait_recv()
        out_ref[...] = part[z] + v["sib_part"][z]
        for c in range(CH):
            r = pl.ds(c * piece, piece)

            @pl.when(has_prev)
            def _():
                cr_copy(z, c).wait_recv()
                out_ref[r, :] = out_ref[r, :] + v["rsum"][z, r, :]

            @pl.when(z > 0)
            def _():
                fi_copy(c).wait_recv()
                out_ref[r, :] = out_ref[r, :] + fin[r, :]

    @pl.when(is1)
    def _():
        own_copy(0).wait_send()
        own_copy(1).wait_send()

    @pl.when(jnp.logical_and(is0, has_prev))
    def _():
        for c in range(CH):
            fi_copy(c).wait_send()

    pl.when(feeds)(lambda: tm_copy().wait_send())
    pl.when(fed)(lambda: gt_copy().wait_send())
    for p in range(spread):

        @pl.when(crossed)
        def _():
            fx_first(p).wait_send()

        @pl.when(cross)
        def _():
            bx_first(p).wait_send()

        @pl.when(tm == near[p])
        def _():
            fx_third(p).wait_send()
            bx_second(p).wait_send()

        if p:

            @pl.when(tm == far[p])
            def _():
                fx_second(p).wait_send()
                bx_third(p).wait_send()

    @pl.when(active)
    def _():
        for k in range(4):
            mx_send(k).wait_send()
        for k in range(6):
            gx_copy(k).wait_send()

    def drain(i, carry):
        b = blk(i)
        pl.when(jnp.where(is0, b <= z, b > z))(lambda: pe_copy(b).wait_send())
        pl.when(i < place)(lambda: sib_copy(b).wait_send())
        for c in range(CH):
            pl.when(jnp.logical_and(has_next, i <= place))(lambda: zr_copy(place - i, c, b).wait_send())
            pl.when(i > place)(lambda: cr_copy(b, c).wait_send())
        return carry

    lax.fori_loop(0, nz, drain, 0)


def local(dims, particles, source_pots, target_pots):
    times, nx, nz, rows, feats = dims
    half = rows // 2
    spread = times // 4
    dma = pltpu.SemaphoreType.DMA
    shapes = [
        ((nz, rows + 16, feats), F32),
        ((nx, rows + 16, feats), F32),
        ((nx * rows, feats), BF16),
        ((nx * rows, feats), BF16),
        ((8, nx * rows), F32),
        ((nz, rows, feats), F32),
        ((nz, rows, feats), F32),
        ((nz, rows, feats), F32),
        ((feats, nx * rows), F32),
        ((8, nx * rows), F32),
        ((nx, rows, feats), F32),
        ((2, rows, feats), F32),
        ((2, half, feats), F32),
        ((rows, feats), F32),
        ((rows, feats), F32),
        ((half // 2 + 8, feats), F32),
        ((rows // spread, feats), F32),
        ((rows, feats), BF16),
        ((rows, feats), BF16),
        ((feats, rows), BF16),
        ((feats, rows), BF16),
        ((rows, half), F32),
    ]
    scratch = [pltpu.VMEM(shape, kind) for shape, kind in shapes]
    line = nz * CH
    for count in (2, line, nz, 0, 4, nz, line, 6, 0, CH, spread, spread):
        kind = dma((count,)) if count else dma
        scratch += [kind, kind]
    out = pl.pallas_call(
        functools.partial(kernel, dims),
        out_shape=jax.ShapeDtypeStruct((rows, feats), F32),
        in_specs=[pl.BlockSpec(memory_space=pltpu.VMEM)] * 3,
        out_specs=pl.BlockSpec(memory_space=pltpu.VMEM),
        scratch_shapes=scratch,
        compiler_params=pltpu.CompilerParams(
            collective_id=0, has_side_effects=True, vmem_limit_bytes=56 * 2**20
        ),
    )(particles[0], source_pots, target_pots)
    return out[None]


def solution(mesh):
    times, nx, nz = mesh.shape["tm"], mesh.shape["row"], mesh.shape["col"]

    def program(particles, source_pots, target_pots):
        rows = particles.shape[1] // (nx * nz)
        dims = (times, nx, nz, rows, particles.shape[2])
        return jax.shard_map(
            functools.partial(local, dims),
            mesh=mesh,
            in_specs=(P("tm", ("row", "col"), None), P("tm", ("row", "col")), P("tm", ("row", "col"))),
            out_specs=P("tm", ("row", "col"), None),
            check_vma=False,
        )(particles, source_pots, target_pots)

    return program
```

time: 92.2 us -> 87 us (0.944)
  the two profiles are of different devices: /device:TPU:352 before, /device:TPU:448 now
where the time goes in v3:
time: 87 us; the launch traced here: 86.8 us
  Pallas kernels  85.1 us (98%)
  local copies, waits for them, and re-layouts  1.67 us (2%)
    pallas_call x1, Pallas kernels, local(): pl.pallas_call(functools.partial(kernel, dims), out_shape=jax.ShapeDtypeS...  85.1 us

profile of v3, /device:TPU:448, one launch (start us, length us, event | category | flops | bytes accessed | tf_op | source)
XLA Modules:
  0.0 86.8 jit_solution(4820009935795481527)
XLA Ops:
  0.0 85.1 %shard_map.37 = f32[256,256]{1,0:T(8,128)} custom-call(f32[256,256]{1,0:T(8,128)} %bitcast.3, f32[1,256]{1,0:T(1,128)} %spot_ref.1, f32[1,256]{1,0:T(1,128)} %tpot_ref.1), custom_call_target="tpu_custom_call" | custom-call | tf_op jit(solution)/shard_map/pallas_call | solution.py:613
  85.2 1.7 %copy.5 = f32[1,256,256]{2,1,0:T(8,128)} copy(f32[1,256,256]{2,1,0:T(8,128)} %bitcast.2) | data formatting | bytes 524288

commit v4 on v3

--- a/solution.py
+++ b/solution.py
@@ -235,12 +235,12 @@
                 pl.when(has_next)(lambda: zr_copy(0, c, z).start())
 
     chain_at = nz + 1
-    near_at, far_at = run, 1
+    near_at, far_at, back_at = run, 1, 15
     wait_m = jnp.where(cross, run + 1, 1)
     mx_step = jnp.where(cross, run + 2, jnp.where(is0, 1, 3))
-    first = jnp.where(cross, nz, jnp.where(is0, 3, 4))
+    first = jnp.where(cross, nz - 1, jnp.where(is0, 3, 4))
     pace = jnp.where(cross, 2, 1)
-    ahead = nz - first
+    ahead = (nz - first) * pace
 
     def order(n):
         k = jnp.where(n < ahead, last - n, n - ahead)
@@ -329,6 +329,15 @@
         return rdma(v["rsum"].at[z, r], fin.at[r], "fi", sib, c)
 
     def step(s, carry):
+        @pl.when(jnp.logical_and(is0, s == back_at))
+        def _():
+            for p in range(spread):
+
+                @pl.when(tm == near[p])
+                def _():
+                    bx_first(p).wait_recv()
+                    bx_second(p).start()
+
         @pl.when(jnp.logical_and(is0, jnp.logical_or(s == far_at, s == near_at)))
         def _():
             for p in range(1, spread):
@@ -478,13 +487,6 @@
             for c in range(CH):
                 cr_copy(z, c).wait_recv()
                 fi_copy(c).start()
-
-        for p in range(spread):
-
-            @pl.when(tm == near[p])
-            def _():
-                bx_first(p).wait_recv()
-                bx_second(p).start()
 
         out_ref[...] = gm[x]
 

time: 87 us -> 83.9 us (0.964)
  Pallas kernels: 85.1 us -> 82.1 us
    pallas_call x1, Pallas kernels: 85.1 us -> 82.1 us  [local(): pl.pallas_call(functools.partial(kernel, dims), out_shape=jax.ShapeDtypeS...]
where the time goes in v4:
time: 83.9 us; the launch traced here: 83.8 us
  Pallas kernels  82.1 us (98%)
  local copies, waits for them, and re-layouts  1.67 us (2%)
    pallas_call x1, Pallas kernels, local(): pl.pallas_call(functools.partial(kernel, dims), out_shape=jax.ShapeDtypeS...  82.1 us

profile of v4, /device:TPU:448, one launch (start us, length us, event | category | flops | bytes accessed | tf_op | source)
XLA Modules:
  0.0 83.8 jit_solution(13518259536560063017)
XLA Ops:
  0.0 82.1 %shard_map.37 = f32[256,256]{1,0:T(8,128)} custom-call(f32[256,256]{1,0:T(8,128)} %bitcast.3, f32[1,256]{1,0:T(1,128)} %spot_ref.1, f32[1,256]{1,0:T(1,128)} %tpot_ref.1), custom_call_target="tpu_custom_call" | custom-call | tf_op jit(solution)/shard_map/pallas_call | solution.py:615
  82.1 1.7 %copy.5 = f32[1,256,256]{2,1,0:T(8,128)} copy(f32[1,256,256]{2,1,0:T(8,128)} %bitcast.2) | data formatting | bytes 524288

commit v5 on v4

--- a/solution.py
+++ b/solution.py
@@ -234,8 +234,8 @@
             for c in (2 * i, 2 * i + 1):
                 pl.when(has_next)(lambda: zr_copy(0, c, z).start())
 
-    chain_at = nz + 1
-    near_at, far_at, back_at = run, 1, 15
+    chain_at = nz
+    near_at, far_at, back_at = run, 1, 14
     wait_m = jnp.where(cross, run + 1, 1)
     mx_step = jnp.where(cross, run + 2, jnp.where(is0, 1, 3))
     first = jnp.where(cross, nz - 1, jnp.where(is0, 3, 4))
@@ -439,7 +439,7 @@
 
                 cr_copy(t, c).start()
 
-        done = s - first - nz // pace
+        done = s - first - nz // pace + 1
 
         @pl.when(jnp.logical_and(active, done >= 0))
         def _():

time: 83.9 us -> 80.5 us (0.959)
  Pallas kernels: 82.1 us -> 78.7 us
    pallas_call x1, Pallas kernels: 82.1 us -> 78.7 us  [local(): pl.pallas_call(functools.partial(kernel, dims), out_shape=jax.ShapeDtypeS...]
where the time goes in v5:
time: 80.5 us; the launch traced here: 80.3 us
  Pallas kernels  78.7 us (98%)
  local copies, waits for them, and re-layouts  1.67 us (2%)
    pallas_call x1, Pallas kernels, local(): pl.pallas_call(functools.partial(kernel, dims), out_shape=jax.ShapeDtypeS...  78.7 us
    unnamed x1, local copies, waits for them, and re-layouts  1.67 us

profile of v5, /device:TPU:448, one launch (start us, length us, event | category | flops | bytes accessed | tf_op | source)
XLA Modules:
  0.0 80.3 jit_solution(10662773246842676493)
XLA Ops:
  0.0 78.7 %shard_map.37 = f32[256,256]{1,0:T(8,128)} custom-call(f32[256,256]{1,0:T(8,128)} %bitcast.3, f32[1,256]{1,0:T(1,128)} %spot_ref.1, f32[1,256]{1,0:T(1,128)} %tpot_ref.1), custom_call_target="tpu_custom_call" | custom-call | tf_op jit(solution)/shard_map/pallas_call | solution.py:615
  78.7 1.7 %copy.5 = f32[1,256,256]{2,1,0:T(8,128)} copy(f32[1,256,256]{2,1,0:T(8,128)} %bitcast.2) | data formatting | bytes 524288

commit v6 on v5

--- a/solution.py
+++ b/solution.py
@@ -237,8 +237,8 @@
     chain_at = nz
     near_at, far_at, back_at = run, 1, 14
     wait_m = jnp.where(cross, run + 1, 1)
-    mx_step = jnp.where(cross, run + 2, jnp.where(is0, 1, 3))
-    first = jnp.where(cross, nz - 1, jnp.where(is0, 3, 4))
+    mx_step = jnp.where(cross, run + 2, jnp.where(is0, 2, 3))
+    first = jnp.where(cross, nz - 1, jnp.where(is0, 4, 4))
     pace = jnp.where(cross, 2, 1)
     ahead = (nz - first) * pace
 

time: 80.5 us -> 82.8 us (1.029)
  the two profiles are of different devices: /device:TPU:448 before, /device:TPU:288 now
where the time goes in v6:
time: 82.8 us; the launch traced here: 82.7 us
  Pallas kernels  81 us (98%)
  local copies, waits for them, and re-layouts  1.67 us (2%)
    pallas_call x1, Pallas kernels, local(): pl.pallas_call(functools.partial(kernel, dims), out_shape=jax.ShapeDtypeS...  81 us
    unnamed x1, local copies, waits for them, and re-layouts  1.67 us

profile of v6, /device:TPU:288, one launch (start us, length us, event | category | flops | bytes accessed | tf_op | source)
XLA Modules:
  0.0 82.7 jit_solution(1822756322622731488)
XLA Ops:
  0.0 81.0 %shard_map.37 = f32[256,256]{1,0:T(8,128)} custom-call(f32[256,256]{1,0:T(8,128)} %bitcast.3, f32[1,256]{1,0:T(1,128)} %spot_ref.1, f32[1,256]{1,0:T(1,128)} %tpot_ref.1), custom_call_target="tpu_custom_call" | custom-call | tf_op jit(solution)/shard_map/pallas_call | solution.py:615
  81.0 1.7 %copy.5 = f32[1,256,256]{2,1,0:T(8,128)} copy(f32[1,256,256]{2,1,0:T(8,128)} %bitcast.2) | data formatting | bytes 524288
